TPU v7x, 32 devices: a whole 2x2x4 slice. The times are simulated.
32 devices in a mesh: rows: 8 (over z, y), cols: 4 (over x, core).
Axes of the slice: x: 2, y: 2, z: 4, core: 2. Of those that a mesh axis runs over, the one named last changes fastest.
Arguments:
- features: bfloat16 [2048, 512], P(('rows', 'cols')), may hold values from -6 to 6
- w_query: bfloat16 [512, 512], replicated, may hold values from -0.25 to 0.25
- w_key: bfloat16 [512, 512], replicated, may hold values from -0.25 to 0.25
- w_value: bfloat16 [512, 512], replicated, may hold values from -0.25 to 0.25
- cotangent: bfloat16 [2048, 512], P(('rows', 'cols')), may hold values from -6 to 6
- block_pairs: int32 [8, 4, 6, 2], P('rows', 'cols'), may hold values from 0 to 3, as said below
- pair_count: int32 [8, 4], P('rows', 'cols'), may hold values from 1 to 6, as said below
- edge_mask: int32 [8, 4, 6, 128, 128], P('rows', 'cols'), may hold values 0 or 1
Outputs:
- attended: bfloat16 [2048, 512], P(('rows', 'cols'))
- input_grad: float32 [2048, 512], P(('rows', 'cols'))
Inputs may be any that keep to these rules, and one draw needn't show every extreme that they name: `block_pairs`: each device's list holds distinct pairs; column 0 is a row block below 2, column 1 a column block below 4. `pair_count`: some device's count equals 6 in every draw.
All inputs are finite; a program needn't handle non-finite values. No bound on the sum of `edge_mask` on one device may be relied on, other than what follows from the above.
Results may differ from a plain program's by a relative error of at most 0.0068.
Values may be sent and summed in bfloat16 or wider, within the bound.
A program may use at most 128 MiB of HBM per device.

v0:
```python
import math

import jax
import jax.numpy as jnp
from jax import lax
from jax.sharding import PartitionSpec as P

HEADS = 8


SCORE_BOUND = 4.0


def project(features, weight):
    return jnp.dot(features, weight, preferred_element_type=jnp.float32).astype(jnp.bfloat16)


def rounded(values):
    return lax.optimization_barrier(values.astype(jnp.bfloat16)).astype(jnp.float32)


def heads_of(table, head_count):
    return table.reshape(table.shape[:-1] + (head_count, table.shape[-1] // head_count))


def edge_terms(query_rows, key_rows, mask_rows, head_count):
    head_size = query_rows.shape[-1] // head_count
    score = jnp.einsum(
        "gihd,gjhd->ghij",
        heads_of(query_rows, head_count),
        heads_of(key_rows, head_count),
        preferred_element_type=jnp.float32,
    )
    bounded = jnp.tanh(score * (1.0 / (math.sqrt(head_size) * SCORE_BOUND)))
    weight = mask_rows.astype(jnp.float32)[:, None] * jnp.exp(SCORE_BOUND * bounded)
    return (weight, bounded)


def self_terms(query, keyed, head_count):
    head_size = query.shape[-1] // head_count
    score = jnp.sum(
        heads_of(query.astype(jnp.float32), head_count)
        * heads_of(keyed.astype(jnp.float32), head_count),
        axis=2,
    )
    bounded = jnp.tanh(score * (1.0 / (math.sqrt(head_size) * SCORE_BOUND)))
    return (jnp.exp(SCORE_BOUND * bounded), bounded)


def add_rows(table, addend, first_row):
    current = lax.dynamic_slice_in_dim(table, first_row, addend.shape[0], 0)
    return lax.dynamic_update_slice_in_dim(table, current + addend, first_row, 0)


def local(features, w_query, w_key, w_value, cotangent, block_pairs, pair_count, edge_mask):
    owned, feature_width = features.shape
    head_count = HEADS
    head_size = feature_width // head_count
    block_size = edge_mask.shape[3]
    column_count = lax.axis_size("cols")
    row_count = lax.axis_size("rows")
    my_column = lax.axis_index("cols")
    part_rows = owned * column_count
    row_blocks = part_rows // block_size
    column_blocks = owned * row_count // block_size
    slot_total = block_pairs.shape[2]
    group_size = math.gcd(slot_total, 8)
    pair_list = block_pairs[0, 0]
    mask_list = edge_mask[0, 0]
    pair_total = pair_count[0, 0]
    turn_total = (pair_total + group_size - 1) // group_size
    inverse_root = 1.0 / math.sqrt(head_size)
    own_first = my_column * owned
    query = project(features, w_query)
    keyed = project(features, w_key)
    valued = project(features, w_value)
    row_query, row_grad = (
        lax.all_gather(query, "cols", axis=0, tiled=True),
        lax.all_gather(cotangent, "cols", axis=0, tiled=True),
    )
    key_cols, value_cols = (
        lax.all_gather(keyed, "rows", axis=0, tiled=True),
        lax.all_gather(valued, "rows", axis=0, tiled=True),
    )
    query_blocks = row_query.reshape(row_blocks, block_size, feature_width)
    grad_blocks = row_grad.reshape(row_blocks, block_size, feature_width)
    key_blocks = key_cols.reshape(column_blocks, block_size, feature_width)
    value_blocks = value_cols.reshape(column_blocks, block_size, feature_width)

    def group_inputs(position):
        first_slot = position * group_size
        pair_rows = lax.dynamic_slice_in_dim(pair_list, first_slot, group_size, 0)
        mask_rows = lax.dynamic_slice_in_dim(mask_list, first_slot, group_size, 0)
        live_slots = first_slot + jnp.arange(group_size, dtype=jnp.int32) < pair_total
        mask_rows = mask_rows * live_slots.astype(jnp.int32)[:, None, None]
        return (pair_rows[:, 0], pair_rows[:, 1], mask_rows)

    def forward_group(position, totals):
        numerator, denominator = totals
        row_index, column_index, mask_rows = group_inputs(position)
        weight, bounded = edge_terms(
            query_blocks[row_index], key_blocks[column_index], mask_rows, head_count
        )
        value_heads = heads_of(value_blocks[column_index], head_count)
        numerator_part = jnp.einsum(
            "ghij,gjhd->gihd",
            weight.astype(jnp.bfloat16),
            value_heads,
            preferred_element_type=jnp.float32,
        )
        numerator = numerator.at[row_index].add(
            numerator_part.reshape(group_size, block_size, feature_width)
        )
        denominator = denominator.at[row_index].add(jnp.sum(weight, axis=3).transpose(0, 2, 1))
        return (numerator, denominator)

    start_sums = (
        jnp.zeros((row_blocks, block_size, feature_width), jnp.float32),
        jnp.zeros((row_blocks, block_size, head_count), jnp.float32),
    )
    numerator, denominator = lax.fori_loop(0, turn_total, forward_group, start_sums)
    self_weight, self_bound = self_terms(query, keyed, head_count)
    value_own = heads_of(valued.astype(jnp.float32), head_count)
    self_part = (rounded(self_weight)[:, :, None] * value_own).reshape(owned, feature_width)
    numerator_flat = add_rows(numerator.reshape(part_rows, feature_width), self_part, own_first)
    denominator_flat = add_rows(denominator.reshape(part_rows, head_count), self_weight, own_first)
    grad_own = heads_of(cotangent.astype(jnp.float32), head_count)
    own_numerator, own_denominator = (
        lax.psum_scatter(numerator_flat, "cols", scatter_dimension=0, tiled=True),
        lax.psum_scatter(denominator_flat, "cols", scatter_dimension=0, tiled=True),
    )
    own_inverse = 1.0 / own_denominator
    own_out = heads_of(own_numerator, head_count) * own_inverse[:, :, None]
    own_delta = jnp.sum(grad_own * own_out, axis=2)
    attended = own_out.reshape(owned, feature_width).astype(jnp.bfloat16)
    row_inverse, row_delta = (
        lax.all_gather(own_inverse, "cols", axis=0, tiled=True),
        lax.all_gather(own_delta, "cols", axis=0, tiled=True),
    )
    inverse_blocks = row_inverse.reshape(row_blocks, block_size, head_count)
    delta_blocks = row_delta.reshape(row_blocks, block_size, head_count)

    def backward_group(position, totals):
        query_grad, range_grad = totals
        row_index, column_index, mask_rows = group_inputs(position)
        query_rows = query_blocks[row_index]
        key_rows = key_blocks[column_index]
        weight, bounded = edge_terms(query_rows, key_rows, mask_rows, head_count)
        query_heads = heads_of(query_rows, head_count)
        key_heads = heads_of(key_rows, head_count)
        value_heads = heads_of(value_blocks[column_index], head_count)
        grad_heads = heads_of(grad_blocks[row_index], head_count)
        grad_value = jnp.einsum(
            "gihd,gjhd->ghij", grad_heads, value_heads, preferred_element_type=jnp.float32
        )
        scaled = weight * inverse_blocks[row_index].transpose(0, 2, 1)[..., None]
        delta_rows = delta_blocks[row_index].transpose(0, 2, 1)[..., None]
        grad_score = (
            scaled * (grad_value - delta_rows) * (1.0 - bounded * bounded) * inverse_root
        ).astype(jnp.bfloat16)
        value_share = scaled.astype(jnp.bfloat16)
        query_part = jnp.einsum(
            "ghij,gjhd->gihd", grad_score, key_heads, preferred_element_type=jnp.float32
        )
        key_part = jnp.einsum(
            "ghij,gihd->gjhd", grad_score, query_heads, preferred_element_type=jnp.float32
        )
        value_part = jnp.einsum(
            "ghij,gihd->gjhd", value_share, grad_heads, preferred_element_type=jnp.float32
        )
        query_grad = query_grad.at[row_index].add(
            query_part.reshape(group_size, block_size, feature_width)
        )
        both_parts = jnp.concatenate(
            [
                key_part.reshape(group_size, block_size, feature_width),
                value_part.reshape(group_size, block_size, feature_width),
            ],
            axis=2,
        )
        range_grad = range_grad.at[column_index].add(both_parts)
        return (query_grad, range_grad)

    start_grads = (
        jnp.zeros((row_blocks, block_size, feature_width), jnp.float32),
        jnp.zeros((column_blocks, block_size, 2 * feature_width), jnp.float32),
    )
    query_grad, range_grad = lax.fori_loop(0, turn_total, backward_group, start_grads)
    own_query_grad = lax.psum_scatter(
        query_grad.reshape(part_rows, feature_width).astype(jnp.bfloat16),
        "cols",
        scatter_dimension=0,
        tiled=True,
    ).astype(jnp.float32)
    self_scaled = self_weight * own_inverse
    self_value_dot = jnp.sum(grad_own * value_own, axis=2)
    self_grad = rounded(
        self_scaled * (self_value_dot - own_delta) * (1.0 - self_bound * self_bound) * inverse_root
    )
    self_share = rounded(self_scaled)
    query_own = heads_of(query.astype(jnp.float32), head_count)
    key_own = heads_of(keyed.astype(jnp.float32), head_count)
    query_total = own_query_grad + (self_grad[:, :, None] * key_own).reshape(owned, feature_width)
    key_self = (self_grad[:, :, None] * query_own).reshape(owned, feature_width)
    value_self = (self_share[:, :, None] * grad_own).reshape(owned, feature_width)
    stacked_weights = jnp.concatenate(
        [w_query.astype(jnp.float32).T, w_key.astype(jnp.float32).T, w_value.astype(jnp.float32).T],
        axis=0,
    )
    own_range = lax.psum_scatter(
        range_grad.reshape(owned * row_count, 2 * feature_width),
        "rows",
        scatter_dimension=0,
        tiled=True,
    )
    key_total = own_range[:, :feature_width] + key_self
    value_total = own_range[:, feature_width:] + value_self
    all_grads = jnp.concatenate([query_total, key_total, value_total], axis=1)
    input_grad = jnp.dot(all_grads, stacked_weights, precision=lax.Precision.HIGHEST)
    return (attended, input_grad)


def solution(mesh):
    in_specs = (
        P(("rows", "cols"), None),
        P(),
        P(),
        P(),
        P(("rows", "cols"), None),
        P("rows", "cols", None, None),
        P("rows", "cols"),
        P("rows", "cols", None, None, None),
    )
    out_specs = (P(("rows", "cols"), None), P(("rows", "cols"), None))
    return jax.shard_map(local, mesh=mesh, in_specs=in_specs, out_specs=out_specs, check_vma=False)
```

profile of v0, /device:TPU:0, one launch (start us, length us, event | category | flops | bytes accessed | tf_op | source)
XLA Modules:
  0.0 313.2 jit_solution(8815302298473349535)
XLA Ops:
  8.0 1.2 convolution_convert_fusion.1
  9.3 1.3 convolution_convert_fusion.2
  10.6 7.2 %all_gather.19 = bf16[256,512]{1,0:T(8,128)(2,1)S(1)} all-gather(bf16[64,512]{1,0:T(8,128)(2,1)S(1)} %convolution_convert_fusion.1), channel_id=1, replica_groups=mesh['rows'=8,'cols'=4] {'cols'}, dimensions={0}, use_global_device_ids=true | all-gather | bytes 327680 | tf_op jit(solution)/shard_map/all_gather | solution.py:78
  17.8 1.2 convert_multiply_fusion.1
  19.3 33.7 %all_gather.20 = bf16[512,512]{1,0:T(8,128)(2,1)} all-gather(bf16[64,512]{1,0:T(8,128)(2,1)S(1)} %get-tuple-element.298), channel_id=1, replica_groups=mesh['rows'=8,'cols'=4] {'rows'}, dimensions={0}, use_global_device_ids=true | all-gather | bytes 589824 | tf_op jit(solution)/shard_map/all_gather | solution.py:82
  53.0 33.2 %all_gather.18 = bf16[512,512]{1,0:T(8,128)(2,1)} all-gather(bf16[64,512]{1,0:T(8,128)(2,1)S(1)} %convolution_convert_fusion.2), channel_id=1, replica_groups=mesh['rows'=8,'cols'=4] {'rows'}, dimensions={0}, use_global_device_ids=true | all-gather | bytes 589824 | tf_op jit(solution)/shard_map/all_gather | solution.py:83
  86.3 8.7 %while.24 = (s32[]{:T(128)}, f32[2,128,512]{2,1,0:T(8,128)S(1)}, f32[2,128,8]{1,2,0:T(8,128)S(1)}, s32[]{:T(128)}, s32[6,2]{0,1:T(2,128)S(1)}, /*index=5*/bf16[4...) while((s32[]{:T(128)}, f32[2,128,512]{2,1,0:T(8,128)S(1)}, ...), condition=%wide.region_4.5_spmd, body=%wide.region_0.4_spmd.sunk | while | flops 68618264 | bytes 9085259 | solution.py:121
  87.1 0.9 constant_dynamic-slice_fusion.7
  88.9 1.6 gather_fusion.2
  91.9 1.6 gather_fusion
  94.1 0.8 scatter_fusion
  95.3 0.8 copy.109
  96.5 0.8 copy-done.1
  97.6 5.8 %all_gather.22 = bf16[256,512]{1,0:T(8,128)(2,1)S(1)} all-gather(bf16[64,512]{1,0:T(8,128)(2,1)S(1)} %copy-done.6), channel_id=1, replica_groups=mesh['rows'=8,'cols'=4] {'cols'}, dimensions={0}, use_global_device_ids=true | all-gather | bytes 327680 | tf_op jit(solution)/shard_map/all_gather | solution.py:79
  103.4 25.2 %reduce-scatter.13.cloned.1.call-done = f32[64,8]{1,0:T(8,128)} async-done(((f32[256,8]{1,0:T(8,128)}), f32[64,8]{1,0:T(8,128)}) %reduce-scatter.13.cloned.1.call-update) | async-done | bytes 2064
  128.6 0.8 copy.110
  129.5 23.4 %reduce-scatter.7.cloned.1.call-done = f32[64,512]{1,0:T(8,128)} async-done(((f32[256,512]{1,0:T(8,128)}), f32[64,512]{1,0:T(8,128)}) %reduce-scatter.7.cloned.1.call-update) | async-done | bytes 131088 | tf_op jit(solution)/shard_map/reduce_scatter | solution.py:129
  152.9 1.0 reshape.120
  154.4 5.2 %all-gather.1 = f32[4,64,8]{1,2,0:T(8,128)S(1)} all-gather(f32[1,64,8]{1,2,0:T(8,128)S(1)} %copy.100), channel_id=1, replica_groups=mesh['rows'=8,'cols'=4] {'cols'}, dimensions={0}, use_global_device_ids=true | all-gather | bytes 10240 | tf_op jit(solution)/shard_map/all_gather | solution.py:138
  160.3 5.2 %all-gather = f32[4,64,8]{1,2,0:T(8,128)S(1)} all-gather(f32[1,64,8]{1,2,0:T(8,128)S(1)} %get-tuple-element.294), channel_id=1, replica_groups=mesh['rows'=8,'cols'=4] {'cols'}, dimensions={0}, use_global_device_ids=true | all-gather | bytes 10240 | tf_op jit(solution)/shard_map/all_gather | solution.py:137
  165.6 1.6 broadcast_in_dim.5
  167.2 15.1 %while.25 = (s32[]{:T(128)}, f32[2,128,512]{2,1,0:T(8,128)S(1)}, f32[4,128,1024]{2,1,0:T(8,128)}, s32[]{:T(128)}, s32[6,2]{0,1:T(2,128)S(1)}, /*index=5*/bf16[4,...) while((s32[]{:T(128)}, f32[2,128,512]{2,1,0:T(8,128)S(1)}, ...), condition=%wide.region_12.13_spmd, body=%wide.region_9.12_spmd.sunk | while | flops 172427296 | bytes 24969652 | solution.py:188
  169.1 1.0 multiply_convert_fusion.7
  170.1 1.6 gather_fusion.5
  171.8 1.6 gather_fusion.3
  175.5 1.0 fusion.105
  178.2 0.8 scatter_fusion.2
  179.3 3.0 scatter_fusion.3
  185.3 46.4 %reduce-scatter.9.cloned.1.call-done = bf16[64,512]{1,0:T(8,128)(2,1)} async-done(((bf16[256,512]{1,0:T(8,128)(2,1)}), bf16[64,512]{1,0:T(8,128)(2,1)}) %reduce-scatter.9.cloned.1.call-update) | async-done | bytes 65552 | tf_op jit(solution)/shard_map/reduce_scatter | solution.py:189
  231.7 71.6 %reduce-scatter.11.cloned.1.call-done = f32[64,1024]{1,0:T(8,128)} async-done(((f32[512,1024]{1,0:T(8,128)}), f32[64,1024]{1,0:T(8,128)}) %reduce-scatter.11.cloned.1.call-update) | async-done | bytes 262160 | tf_op jit(solution)/shard_map/reduce_scatter | solution.py:210
  303.4 1.0 fusion.33
  304.4 2.2 fusion.22
  (110 shorter events, 15.3 us)
Async XLA Ops:
  7.2 0.8 copy-start
  7.2 121.4 %reduce-scatter.13.cloned.1.call-start = ((), (), s32[]{:S(2)}) async-start(), calls=%async_computation.7 | async-start | bytes 163840
  9.3 9.8 %copy-start.4 = (bf16[64,512]{1,0:T(8,128)(2,1)}, bf16[64,512]{1,0:T(8,128)(2,1)S(1)}, u32[]{:S(2)}) copy-start(bf16[64,512]{1,0:T(8,128)(2,1)S(1)} %convolution_convert_fusion.1) | copy-start | bytes 196612
  9.3 77.0 %copy-start.14 = (s32[1,1,6,2]{2,3,1,0:T(2,128)S(1)}, s32[1,1,6,2]{2,3,1,0:T(2,128)}, u32[]{:S(2)}) copy-start(s32[1,1,6,2]{2,3,1,0:T(2,128)} %param.17) | copy-start | bytes 148
  19.0 67.2 %copy-start.8 = (bf16[64,512]{1,0:T(8,128)(2,1)}, bf16[64,512]{1,0:T(8,128)(2,1)S(1)}, u32[]{:S(2)}) copy-start(bf16[64,512]{1,0:T(8,128)(2,1)S(1)} %get-tuple-element.298) | copy-start | bytes 196612
  95.0 2.5 copy-start.6
  96.1 56.8 %reduce-scatter.7.cloned.1.call-start = ((), (), s32[]{:S(2)}) async-start(), calls=%async_computation.4 | async-start | bytes 655360 | tf_op jit(solution)/shard_map/reduce_scatter | solution.py:129
  96.5 0.8 copy-start.1
  97.3 134.4 %reduce-scatter.9.cloned.1.call-start = ((), (), s32[]{:S(2)}) async-start(), calls=%async_computation.5 | async-start | bytes 327680 | tf_op jit(solution)/shard_map/reduce_scatter | solution.py:189
  167.2 7.8 %copy-start.2 = (bf16[2,128,512]{2,1,0:T(8,128)(2,1)}, bf16[2,128,512]{2,1,0:T(8,128)(2,1)S(1)}, u32[]{:S(2)}) copy-start(bf16[2,128,512]{2,1,0:T(8,128)(2,1)S(1)} %get-tuple-element.549) | copy-start | bytes 786436 | tf_op jit(solution)/shard_map/while
  179.3 3.1 copy-start.3
  182.3 1.6 copy-start.15
  183.1 120.3 %reduce-scatter.11.cloned.1.call-start = ((), (), s32[]{:S(2)}) async-start(), calls=%async_computation.6 | async-start | bytes 2359296 | tf_op jit(solution)/shard_map/reduce_scatter | solution.py:210
  183.2 1.5 copy-start.12
  183.2 120.2 %copy-start.5 = (bf16[64,512]{1,0:T(8,128)(2,1)S(1)}, bf16[64,512]{1,0:T(8,128)(2,1)}, u32[]{:S(2)}) copy-start(bf16[64,512]{1,0:T(8,128)(2,1)} %copy-done.4) | copy-start | bytes 196612
  183.2 120.2 %copy-start.7 = (bf16[64,512]{1,0:T(8,128)(2,1)S(1)}, bf16[64,512]{1,0:T(8,128)(2,1)}, u32[]{:S(2)}) copy-start(bf16[64,512]{1,0:T(8,128)(2,1)} %param.16) | copy-start | bytes 196612
  183.2 120.2 %copy-start.9 = (bf16[64,512]{1,0:T(8,128)(2,1)S(1)}, bf16[64,512]{1,0:T(8,128)(2,1)}, u32[]{:S(2)}) copy-start(bf16[64,512]{1,0:T(8,128)(2,1)} %copy-done.8) | copy-start | bytes 196612
  183.7 120.7 %copy-start.10 = (bf16[512,512]{1,0:T(8,128)(2,1)S(1)}, bf16[512,512]{1,0:T(8,128)(2,1)}, u32[]{:S(2)}) copy-start(bf16[512,512]{1,0:T(8,128)(2,1)} %param.15) | copy-start | bytes 1572868
  183.7 120.7 %copy-start.11 = (bf16[512,512]{1,0:T(8,128)(2,1)S(1)}, bf16[512,512]{1,0:T(8,128)(2,1)}, u32[]{:S(2)}) copy-start(bf16[512,512]{1,0:T(8,128)(2,1)} %param.13) | copy-start | bytes 1572868
  183.7 120.7 %copy-start.13 = (bf16[512,512]{1,0:T(8,128)(2,1)S(1)}, bf16[512,512]{1,0:T(8,128)(2,1)}, u32[]{:S(2)}) copy-start(bf16[512,512]{1,0:T(8,128)(2,1)} %param.14) | copy-start | bytes 1572868
Sparse Core Ops, SparseCore 0:
  96.2 32.3 reduce-scatter.12
  131.2 21.6 reduce-scatter.6
  183.2 48.4 reduce-scatter.8
  235.5 67.8 reduce-scatter.10
where the time goes:
time: 316 us; the launch traced here: 313 us
  waiting for transfers between devices  167 us (53%)
  blocking collectives  90.2 us (29%)
  local copies, waits for them, and re-layouts  19.9 us (6%)
  between operations  14.7 us (5%)
  other arithmetic  11.3 us (4%)
  matrix products  9.36 us (3%)
    reduce_scatter x1, waiting for transfers between devices, local(): lax.psum_scatter(range_grad.reshape(owned * row_count, 2 * feature_width)...  71.6 us
    reduce_scatter x1, waiting for transfers between devices, local(): lax.psum_scatter(query_grad.reshape(part_rows, feature_width).astype(jnp....  46.4 us
    all_gather x1, blocking collectives, local(): lax.all_gather(keyed, 'rows', axis=0, tiled=True)  33.7 us
    all_gather x1, blocking collectives, local(): lax.all_gather(valued, 'rows', axis=0, tiled=True)  33.2 us
    unnamed x5, waiting for transfers between devices  25.7 us
    reduce_scatter x1, waiting for transfers between devices, local(): lax.psum_scatter(numerator_flat, 'cols', scatter_dimension=0, tiled=True)  23.4 us
    all_gather x1, blocking collectives, local(): lax.all_gather(query, 'cols', axis=0, tiled=True)  7.19 us
  transfers between devices with their start and end apart: 4, of which 4 were waited for; matrix products, arithmetic and copies ran while one was open for 1% of the time, Pallas kernels for 0%

commit v1 on v0

v1 whole, which is shorter than its diff:
```python
import functools
import math

import jax
import jax.numpy as jnp
from jax import lax
from jax.experimental import pallas as pl
from jax.experimental.pallas import tpu as pltpu
from jax.sharding import PartitionSpec as P

HEADS = 8
SCORE_BOUND = 4.0
LANES = 128
MESH = pl.DeviceIdType.MESH
F32 = jnp.float32
BF16 = jnp.bfloat16


def dot(a, b):
    return jnp.dot(a, b, preferred_element_type=F32)


def dot_t(a, b):
    return lax.dot_general(a, b, (((1,), (1,)), ((), ())), preferred_element_type=F32)


def kernel(
    row_total, col_total, keep,
    feat, wq, wk, wv, cot, pairs, count, mask,
    att_out, grad_out,
    fcol, frow, crow, k_s, v_s, kt_s, vt_s, q_s, qtm, ctm, mask_t, e_s, t_s,
    num_t, den_s, inv_s, dl_s, qg_t, kg_s, vg_s,
    stat_send, stat_recv, num_send, num_recv, qg_send, qg_recv, rg_send, rg_recv,
    col_ss, col_rs, fr_ss, fr_rs, cr_ss, cr_rs, st_ss, st_rs, nu_ss, nu_rs,
    qg_ss, qg_rs, rg_ss, rg_rs,
):
    owned, width = feat.shape
    slots, block, _ = mask.shape
    head = width // HEADS
    part = owned * col_total
    row_blocks = part // block
    chunks = owned * row_total // block
    per = block // owned
    me_r = lax.axis_index("rows")
    me_c = lax.axis_index("cols")
    scale = 1.0 / (math.sqrt(head) * SCORE_BOUND)
    inverse_root = 1.0 / math.sqrt(head)

    def remote(src, dst, ss, rs, axis, peer):
        return pltpu.make_async_remote_copy(
            src_ref=src, dst_ref=dst, send_sem=ss, recv_sem=rs,
            device_id={axis: peer}, device_id_type=MESH,
        )

    def arrived(buf, ss, rs, axis, src):
        remote(buf.at[src], buf.at[src], ss.at[src], rs.at[src], axis, src).wait_recv()

    row_peers = [lax.rem(me_r + d, row_total) for d in range(1, row_total)]
    col_peers = [lax.rem(me_c + d, col_total) for d in range(1, col_total)]

    barrier = pltpu.get_barrier_semaphore()
    for peer in row_peers:
        pl.semaphore_signal(barrier, inc=1, device_id={"rows": peer}, device_id_type=MESH)
    for peer in col_peers:
        pl.semaphore_signal(barrier, inc=1, device_id={"cols": peer}, device_id_type=MESH)
    pl.semaphore_wait(barrier, row_total + col_total - 2)

    for peer in col_peers:
        remote(feat, frow.at[me_c], fr_ss.at[peer], fr_rs.at[me_c], "cols", peer).start()
    for peer in row_peers:
        remote(feat, fcol.at[me_r], col_ss.at[peer], col_rs.at[me_r], "rows", peer).start()
    for peer in col_peers:
        remote(cot, crow.at[me_c], cr_ss.at[peer], cr_rs.at[me_c], "cols", peer).start()

    fcol[me_r] = feat[...]
    frow[me_c] = feat[...]
    crow[me_c] = cot[...]
    num_t[...] = jnp.zeros_like(num_t)
    den_s[...] = jnp.zeros_like(den_s)
    qg_t[...] = jnp.zeros_like(qg_t)

    live_total = count[0]

    def mask_chunk(k, carry):
        for b in range(row_blocks):
            def find(s, found):
                hit = (pairs[2 * s] == b) & (pairs[2 * s + 1] == k) & (s < live_total)
                return jnp.where(hit, s, found)

            found = lax.fori_loop(0, slots, find, jnp.int32(-1), unroll=slots <= 8)
            live = (found >= 0).astype(F32)
            tile = mask[jnp.maximum(found, 0)].astype(F32) * live
            j = lax.broadcasted_iota(jnp.int32, (block, block), 0) + k * block
            i = lax.broadcasted_iota(jnp.int32, (block, block), 1) + b * block
            own = i - me_c * owned
            same = (own == j - me_r * owned) & (own >= 0) & (own < owned)
            first = pl.multiple_of(k * block, block)
            mask_t[pl.ds(first, block), b * block:(b + 1) * block] = tile.T + same.astype(F32)
        return carry

    lax.fori_loop(0, chunks, mask_chunk, 0)

    for peer in col_peers:
        arrived(frow, fr_ss, fr_rs, "cols", peer)
    query = dot(frow[...].reshape(part, width), wq[...])
    q_s[...] = query.astype(BF16)
    query_t = query.T.astype(BF16)
    for h in range(HEADS):
        low, high = (h % 2) * head, (h % 2 + 1) * head
        other = head - low
        qtm[h, low:high, :] = query_t[h * head:(h + 1) * head, :]
        qtm[h, other:other + head, :] = jnp.zeros((head, part), BF16)

    own_chunk = me_r // per

    def terms(h, kp, m):
        t = jnp.tanh(dot(kp, qtm[h]) * scale)
        return m * jnp.exp(SCORE_BOUND * t), t

    def forward(step, carry):
        k = lax.rem(own_chunk + step, chunks)
        first = pl.multiple_of(k * block, block)
        for o in range(per):
            src = k * per + o

            @pl.when(src != me_r)
            def _():
                arrived(fcol, col_ss, col_rs, "rows", src)
        rows = fcol[pl.ds(k * per, per)].reshape(block, width)
        keyed = dot(rows, wk[...])
        k_s[pl.ds(first, block), :] = keyed.astype(BF16)
        kt_s[k] = keyed.T.astype(BF16)
        valued = dot(rows, wv[...])
        v_s[pl.ds(first, block), :] = valued.astype(BF16)
        vt_s[k] = valued.T.astype(BF16)

        def pair(p, inner):
            kp = k_s[pl.ds(first, block), pl.ds(pl.multiple_of(p * LANES, LANES), LANES)]
            m = mask_t[pl.ds(first, block), :]
            for a in range(2):
                h = 2 * p + a
                e, t = terms(h, kp, m)
                if keep:
                    e_s[h, pl.ds(first, block), :] = e
                    t_s[h, pl.ds(first, block), :] = t
                vt = vt_s[k, pl.ds(pl.multiple_of(h * head, head), head), :]
                num_t[h] += dot(vt, e.astype(BF16))
                den_s[h] += jnp.sum(e.reshape(block // 8, 8, part), axis=0)
            return inner

        lax.fori_loop(0, HEADS // 2, pair, 0)
        return carry

    lax.fori_loop(0, chunks, forward, 0)

    for peer in col_peers:
        arrived(crow, cr_ss, cr_rs, "cols", peer)
    grad_t = crow[...].reshape(part, width).astype(F32).T
    for h in range(HEADS):
        low, high = (h % 2) * head, (h % 2 + 1) * head
        other = head - low
        ctm[h, low:high, :] = grad_t[h * head:(h + 1) * head, :].astype(BF16)
        ctm[h, other:other + head, :] = jnp.zeros((head, part), BF16)

    stat_send[0] = jnp.sum(den_s[...], axis=1)
    stat_send[1] = jnp.sum(num_t[...] * grad_t.reshape(HEADS, head, part), axis=1)
    for peer in col_peers:
        remote(stat_send, stat_recv.at[me_c], st_ss.at[peer], st_rs.at[me_c], "cols", peer).start()
    stat_recv[me_c] = stat_send[...]
    for peer in col_peers:
        arrived(stat_recv, st_ss, st_rs, "cols", peer)
    total = jnp.sum(stat_recv[...], axis=0)
    inverse = 1.0 / total[0]
    inv_s[...] = inverse
    dl_s[...] = total[1] * inverse

    out_part = (num_t[...] * inverse[:, None, :]).reshape(width, part).T
    num_send[...] = out_part.astype(BF16).reshape(col_total, owned, width)
    for peer in col_peers:
        remote(num_send.at[peer], num_recv.at[me_c], nu_ss.at[peer], nu_rs.at[me_c], "cols", peer).start()
    num_recv[me_c] = num_send[me_c]

    lane = lax.broadcasted_iota(jnp.int32, (part, LANES), 1)

    def backward(step, carry):
        k = lax.rem(own_chunk + step + 1, chunks)
        first = pl.multiple_of(k * block, block)

        def pair(p, inner):
            lanes = pl.ds(pl.multiple_of(p * LANES, LANES), LANES)
            vp = v_s[pl.ds(first, block), lanes]
            qp = q_s[:, lanes]
            cp = crow[:, :, lanes].reshape(part, LANES)
            kg = jnp.zeros((block, LANES), F32)
            vg = jnp.zeros((block, LANES), F32)
            for a in range(2):
                h = 2 * p + a
                if keep:
                    e, t = e_s[h, pl.ds(first, block), :], t_s[h, pl.ds(first, block), :]
                else:
                    e, t = terms(h, k_s[pl.ds(first, block), lanes], mask_t[pl.ds(first, block), :])
                share = e * inv_s[pl.ds(h, 1), :]
                grad_value = dot(vp, ctm[h])
                g = share * (grad_value - dl_s[pl.ds(h, 1), :]) * ((1.0 - t * t) * inverse_root)
                gb, sb = g.astype(BF16), share.astype(BF16)
                mine = (lane >= a * head) & (lane < (a + 1) * head)
                kt = kt_s[k, pl.ds(pl.multiple_of(h * head, head), head), :]
                qg_t[h] += dot(kt, gb)
                kg += dot(gb, jnp.where(mine, qp, jnp.zeros_like(qp)))
                vg += dot(sb, jnp.where(mine, cp, jnp.zeros_like(cp)))
            kg_s[:, lanes] = kg.astype(BF16)
            vg_s[:, lanes] = vg.astype(BF16)
            return inner

        lax.fori_loop(0, HEADS // 2, pair, 0)
        sums = dot_t(kg_s[...], wk[...]) + dot_t(vg_s[...], wv[...])
        rg_send[pl.ds(k * per, per)] = sums.astype(BF16).reshape(per, owned, width)
        for o in range(per):
            dst = k * per + o

            @pl.when(dst != me_r)
            def _():
                remote(
                    rg_send.at[dst], rg_recv.at[me_r], rg_ss.at[dst], rg_rs.at[me_r], "rows", dst
                ).start()
        return carry

    lax.fori_loop(0, chunks, backward, 0)
    rg_recv[me_r] = rg_send[me_r]

    query_grad = qg_t[...].reshape(width, part).T.astype(BF16)
    qg_send[...] = dot_t(query_grad, wq[...]).astype(BF16).reshape(col_total, owned, width)
    for peer in col_peers:
        remote(qg_send.at[peer], qg_recv.at[me_c], qg_ss.at[peer], qg_rs.at[me_c], "cols", peer).start()
    qg_recv[me_c] = qg_send[me_c]

    for peer in col_peers:
        arrived(num_recv, nu_ss, nu_rs, "cols", peer)
    att_out[...] = jnp.sum(num_recv[...].astype(F32), axis=0).astype(BF16)
    for peer in col_peers:
        arrived(qg_recv, qg_ss, qg_rs, "cols", peer)
    for peer in row_peers:
        arrived(rg_recv, rg_ss, rg_rs, "rows", peer)
    grad_out[...] = jnp.sum(qg_recv[...].astype(F32), axis=0) + jnp.sum(
        rg_recv[...].astype(F32), axis=0
    )

    for peer in col_peers:
        remote(feat, frow.at[me_c], fr_ss.at[peer], fr_rs.at[me_c], "cols", peer).wait_send()
        remote(cot, crow.at[me_c], cr_ss.at[peer], cr_rs.at[me_c], "cols", peer).wait_send()
        remote(stat_send, stat_recv.at[me_c], st_ss.at[peer], st_rs.at[me_c], "cols", peer).wait_send()
        remote(num_send.at[peer], num_recv.at[me_c], nu_ss.at[peer], nu_rs.at[me_c], "cols", peer).wait_send()
        remote(qg_send.at[peer], qg_recv.at[me_c], qg_ss.at[peer], qg_rs.at[me_c], "cols", peer).wait_send()
    for peer in row_peers:
        remote(feat, fcol.at[me_r], col_ss.at[peer], col_rs.at[me_r], "rows", peer).wait_send()
        remote(rg_send.at[peer], rg_recv.at[me_r], rg_ss.at[peer], rg_rs.at[me_r], "rows", peer).wait_send()


def local(row_total, col_total, features, w_query, w_key, w_value, cotangent, block_pairs, pair_count, edge_mask):
    owned, width = features.shape
    slots, block = edge_mask.shape[2], edge_mask.shape[3]
    part = owned * col_total
    span = owned * row_total
    chunks = span // block
    head = width // HEADS
    keep = span <= 512
    kept = (HEADS, span, part) if keep else (1, 8, LANES)
    vmem = pl.BlockSpec(memory_space=pltpu.VMEM)
    smem = pl.BlockSpec(memory_space=pltpu.SMEM)

    def buf(*shape, dtype=BF16):
        return pltpu.VMEM(shape, dtype)

    by_col = buf(col_total, owned, width)
    by_row = buf(row_total, owned, width)
    col_sem = pltpu.SemaphoreType.DMA((col_total,))
    row_sem = pltpu.SemaphoreType.DMA((row_total,))
    scratch = [
        by_row, by_col, by_col,
        buf(span, width), buf(span, width),
        buf(chunks, width, block), buf(chunks, width, block),
        buf(part, width), buf(HEADS, LANES, part), buf(HEADS, LANES, part),
        buf(span, part, dtype=F32), buf(*kept, dtype=F32), buf(*kept, dtype=F32),
        buf(HEADS, head, part, dtype=F32), buf(HEADS, 8, part, dtype=F32),
        buf(HEADS, part, dtype=F32), buf(HEADS, part, dtype=F32),
        buf(HEADS, head, part, dtype=F32), buf(block, width), buf(block, width),
        buf(2, HEADS, part, dtype=F32), buf(col_total, 2, HEADS, part, dtype=F32),
        by_col, by_col, by_col, by_col, by_row, by_row,
        row_sem, row_sem, col_sem, col_sem, col_sem, col_sem, col_sem, col_sem, col_sem, col_sem,
        col_sem, col_sem, row_sem, row_sem,
    ]
    return pl.pallas_call(
        functools.partial(kernel, row_total, col_total, keep),
        out_shape=(
            jax.ShapeDtypeStruct((owned, width), BF16),
            jax.ShapeDtypeStruct((owned, width), F32),
        ),
        in_specs=[vmem, vmem, vmem, vmem, vmem, smem, smem, vmem],
        out_specs=(vmem, vmem),
        scratch_shapes=scratch,
        compiler_params=pltpu.CompilerParams(
            collective_id=0, has_side_effects=True, vmem_limit_bytes=56 * 1024 * 1024
        ),
    )(
        features, w_query, w_key, w_value, cotangent,
        block_pairs.reshape(-1), pair_count.reshape(-1), edge_mask.reshape(slots, block, block),
    )


def solution(mesh):
    in_specs = (
        P(("rows", "cols"), None),
        P(),
        P(),
        P(),
        P(("rows", "cols"), None),
        P("rows", "cols", None, None),
        P("rows", "cols"),
        P("rows", "cols", None, None, None),
    )
    out_specs = (P(("rows", "cols"), None), P(("rows", "cols"), None))
    body = functools.partial(local, mesh.shape["rows"], mesh.shape["cols"])
    return jax.shard_map(body, mesh=mesh, in_specs=in_specs, out_specs=out_specs, check_vma=False)
```

time: 316 us -> 51.8 us (0.16)
  waiting for transfers between devices: 167 us -> 0 us
  blocking collectives: 90.2 us -> 0 us
  Pallas kernels: 0 us -> 46.8 us
  local copies, waits for them, and re-layouts: 19.9 us -> 3.52 us
  between operations: 14.7 us -> 1.3 us
  other arithmetic: 11.3 us -> 0 us
  matrix products: 9.36 us -> 0 us
    reduce_scatter x3 -> x0, waiting for transfers between devices: 141 us -> none  [the longest x1 71.6 us: local(): lax.psum_scatter(range_grad.reshape(owned * row_count, 2 * feature_width)...]
    all_gather x6 -> x0, blocking collectives: 90.2 us -> none  [the longest x1 33.7 us: local(): lax.all_gather(keyed, 'rows', axis=0, tiled=True)]
    pallas_call x0 -> x1, Pallas kernels: none -> 46.8 us  [local(): pl.pallas_call(functools.partial(kernel, row_total, col_total, keep), out...]
    unnamed x5 -> x0, waiting for transfers between devices: 25.7 us -> none
    gather x16 -> x0, local copies, waits for them, and re-layouts: 10.4 us -> none  [the longest x2 1.78 us: forward_group(): key_blocks[column_index]]
    dot_general x11 -> x0, matrix products: 9.36 us -> none  [the longest x3 3.76 us: project(): jnp.dot(features, weight, preferred_element_type=jnp.float32)]
    scatter-add x4 -> x0, other arithmetic: 5.27 us -> none  [the longest x1 3.05 us: backward_group(): range_grad = range_grad.at[column_index].add(both_parts)]
    convert_element_type x7 -> x0, other arithmetic: 4.34 us -> none  [the longest x2 1.3 us: group_inputs(): mask_rows = mask_rows * live_slots.astype(jnp.int32)[:, None, None]]
  transfers between devices with their start and end apart: 4 -> 0, of which waited for: 4 -> 0; matrix products, arithmetic and copies ran while one was open for 1% -> 0% of each run, Pallas kernels for 0% -> 0%
where the time goes in v1:
time: 51.8 us; the launch traced here: 51.6 us
  Pallas kernels  46.8 us (90%)
  local copies, waits for them, and re-layouts  3.52 us (7%)
  between operations  1.3 us (3%)
    pallas_call x1, Pallas kernels, local(): pl.pallas_call(functools.partial(kernel, row_total, col_total, keep), out...  46.8 us
    unnamed x7, local copies, waits for them, and re-layouts  2.93 us

profile of v1, /device:TPU:0, one launch (start us, length us, event | category | flops | bytes accessed | tf_op | source)
XLA Modules:
  0.0 51.6 jit_solution(12175589928937325972)
XLA Ops:
  1.3 0.0 copy-start.1
  1.3 0.7 %copy-done.1 = s32[1,1,6,2]{2,3,1,0:T(2,128)S(1)} copy-done((s32[1,1,6,2]{2,3,1,0:T(2,128)S(1)}, s32[1,1,6,2]{2,3,1,0:T(2,128)}, u32[]{:S(2)}) %copy-start.1) | copy-done | bytes 72
  2.0 0.1 copy.11
  2.0 0.6 %reshape.13.pairs = s32[12]{0:T(128)} reshape(s32[1,1,6,2]{3,2,1,0:T(8,128)S(1)} %copy.11) | data formatting | bytes 96 | tf_op jit(solution)/shard_map/reshape | solution.py:306
  2.6 46.8 %shard_map.95 = (bf16[64,512]{1,0:T(8,128)(2,1)}, f32[64,512]{1,0:T(8,128)}) custom-call(bf16[64,512]{1,0:T(8,128)(2,1)} %feat.1, bf16[512,512]{1,0:T(8,128)(2,1)} %wq.1, bf16[512,512]{1,0:T(8,128)(2,1)} %wk.1, bf16[512,512]{1,0:T(8,128)(2,1)} %wv.1, bf16[64,512]{1,0:T(8,128)(2,1)} %cot.1, s32[12]{0:T(128)} %reshape.13.pairs, s32[1]{0:T(128)} %bitcast.2.count, ...), custom_call_target="tpu_custom_call" | custom-call | tf_op jit(solution)/shard_map/pallas_call | solution.py:292
  49.4 0.0 copy-start
  49.5 1.5 %copy.15 = bf16[64,512]{1,0:T(8,128)(2,1)} copy(bf16[64,512]{1,0:T(8,128)(2,1)} %get-tuple-element.4) | data formatting | bytes 131072
  51.0 0.0 copy-done
  51.0 0.7 %copy.16 = f32[64,512]{1,0:T(8,128)} copy(f32[64,512]{1,0:T(8,128)S(1)} %copy-done) | data formatting | bytes 262144
Async XLA Ops:
  1.3 0.7 %copy-start.1 = (s32[1,1,6,2]{2,3,1,0:T(2,128)S(1)}, s32[1,1,6,2]{2,3,1,0:T(2,128)}, u32[]{:S(2)}) copy-start(s32[1,1,6,2]{2,3,1,0:T(2,128)} %param.13) | copy-start | bytes 148
  49.4 1.5 %copy-start = (f32[64,512]{1,0:T(8,128)S(1)}, f32[64,512]{1,0:T(8,128)}, u32[]{:S(2)}) copy-start(f32[64,512]{1,0:T(8,128)} %get-tuple-element.5) | copy-start | bytes 393220

commit v2 on v1

v2 whole, which is shorter than its diff:
```python
import functools
import math

import jax
import jax.numpy as jnp
from jax import lax
from jax.experimental import pallas as pl
from jax.experimental.pallas import tpu as pltpu
from jax.sharding import PartitionSpec as P

HEADS = 8
SCORE_BOUND = 4.0
LANES = 128
MESH = pl.DeviceIdType.MESH
F32 = jnp.float32
BF16 = jnp.bfloat16


def dot(a, b):
    return jnp.dot(a, b, preferred_element_type=F32)


def dot_t(a, b):
    return lax.dot_general(a, b, (((1,), (1,)), ((), ())), preferred_element_type=F32)


def kernel(
    row_total, col_total, keep,
    feat, wq_in, wk_in, wv_in, cot, pairs, count, mask_in,
    att_out, grad_out,
    wq, wk, wv, mask, fcol, frow, crow, k_s, v_s, kt_s, vt_s, q_s, qtm, ctm, mask_t, e_s, a_s, b_s,
    num_t, den_s, inv_s, dl_s, qg_t, kg_s, vg_s,
    stat_send, stat_recv, num_send, num_recv, qg_send, qg_recv,
    tw_send, tw_recv, rg_own, rg_send, rg_recv,
    load_s, col_ss, col_fs, col_rs, fr_ss, fr_rs, cr_ss, cr_rs, st_ss, st_rs, nu_ss, nu_rs,
    qg_ss, qg_rs, tw_ss, tw_rs, rg_ss, rg_rs,
):
    owned, width = feat.shape
    slots, block, _ = mask.shape
    head = width // HEADS
    part = owned * col_total
    row_blocks = part // block
    chunks = owned * row_total // block
    per = block // owned
    me_r = lax.axis_index("rows")
    me_c = lax.axis_index("cols")
    scale = 1.0 / (math.sqrt(head) * SCORE_BOUND)
    inverse_root = 1.0 / math.sqrt(head)

    def flip(index, amount, count_all):
        if count_all & (count_all - 1):
            return lax.rem(index + amount, count_all)
        out, bit = 0, 1
        while bit < count_all:
            out = out + bit * lax.rem(lax.div(index, bit) + lax.div(jnp.int32(amount), bit), 2)
            bit *= 2
        return out

    me_k, side = lax.div(me_r, per), lax.rem(me_r, per)
    twin_r = me_k * per + (1 - side)
    line = [flip(me_k, d, chunks) for d in range(1, chunks)]
    half, side_c = lax.div(me_c, 2), lax.rem(me_c, 2)
    twin_c = half * 2 + (1 - side_c)
    halves = [lax.rem(half + d, col_total // 2) for d in range(1, col_total // 2)]
    col_line = [x * 2 + side_c for x in halves]
    col_cross = [x * 2 + (1 - side_c) for x in halves]
    col_peers = col_cross + col_line + [twin_c]

    def remote(src, dst, ss, rs, axis, peer):
        return pltpu.make_async_remote_copy(
            src_ref=src, dst_ref=dst, send_sem=ss, recv_sem=rs,
            device_id={axis: peer}, device_id_type=MESH,
        )

    def arrived(buf, ss, rs, axis, src):
        remote(buf.at[src], buf.at[src], ss.at[src], rs.at[src], axis, src).wait_recv()

    loads = [
        pltpu.make_async_copy(src, dst, load_s.at[n])
        for n, (src, dst) in enumerate(
            [
                (mask_in, mask), (feat, frow.at[me_c]), (feat, fcol.at[me_r]), (cot, crow.at[me_c]),
                (wq_in, wq), (wk_in, wk), (wv_in, wv),
            ]
        )
    ]

    barrier = pltpu.get_barrier_semaphore()
    for peer in [twin_r] + [x * per + side for x in line]:
        pl.semaphore_signal(barrier, inc=1, device_id={"rows": peer}, device_id_type=MESH)
    for peer in col_peers:
        pl.semaphore_signal(barrier, inc=1, device_id={"cols": peer}, device_id_type=MESH)
    for load in loads:
        load.start()
    pl.semaphore_wait(barrier, chunks + col_total - 1)

    sends = []

    def send(*args):
        copy = remote(*args)
        copy.start()
        sends.append(copy)

    for peer in col_line:
        send(feat, frow.at[me_c], fr_ss.at[peer], fr_rs.at[me_c], "cols", peer)
    send(feat, fcol.at[me_r], col_fs.at[me_k], col_rs.at[me_r], "rows", twin_r)
    for x in line:
        send(feat, fcol.at[me_r], col_ss.at[x], col_rs.at[me_r], "rows", x * per + side)
    send(feat, frow.at[me_c], fr_ss.at[me_c], fr_rs.at[me_c], "cols", twin_c)
    for peer in col_line:
        send(cot, crow.at[me_c], cr_ss.at[peer], cr_rs.at[me_c], "cols", peer)
    send(cot, crow.at[me_c], cr_ss.at[me_c], cr_rs.at[me_c], "cols", twin_c)

    num_t[...] = jnp.zeros_like(num_t)
    den_s[...] = jnp.zeros_like(den_s)
    qg_t[...] = jnp.zeros_like(qg_t)
    for h in range(HEADS):
        other = (1 - h % 2) * head
        qtm[h, other:other + head, :] = jnp.zeros((head, part), BF16)
        ctm[h, other:other + head, :] = jnp.zeros((head, part), BF16)

    live_total = count[0, 0]
    loads[0].wait()

    def mask_chunk(k, carry):
        for b in range(row_blocks):
            def find(s, found):
                hit = (pairs[s, 0] == b) & (pairs[s, 1] == k) & (s < live_total)
                return jnp.where(hit, s, found)

            found = lax.fori_loop(0, slots, find, jnp.int32(-1), unroll=slots <= 8)
            live = (found >= 0).astype(F32)
            tile = mask[jnp.maximum(found, 0)].astype(F32) * live
            j = lax.broadcasted_iota(jnp.int32, (block, block), 0) + k * block
            i = lax.broadcasted_iota(jnp.int32, (block, block), 1) + b * block
            own = i - me_c * owned
            same = (own == j - me_r * owned) & (own >= 0) & (own < owned)
            first = pl.multiple_of(k * block, block)
            mask_t[pl.ds(first, block), b * block:(b + 1) * block] = tile.T + same.astype(F32)
        return carry

    lax.fori_loop(0, chunks, mask_chunk, 0)

    def share_columns(buf, ss, rs):
        for peer in col_line:
            arrived(buf, ss, rs, "cols", peer)
            send(buf.at[peer], buf.at[peer], ss.at[peer + 1 - 2 * side_c], rs.at[peer], "cols", twin_c)
        for peer in [twin_c] + col_cross:
            arrived(buf, ss, rs, "cols", peer)

    for load in loads[1:5]:
        load.wait()
    share_columns(frow, fr_ss, fr_rs)
    query = dot(frow[...].reshape(part, width), wq[...])
    q_s[...] = query.astype(BF16)
    query_t = query.T.astype(BF16)
    for h in range(HEADS):
        low, high = (h % 2) * head, (h % 2 + 1) * head
        qtm[h, low:high, :] = query_t[h * head:(h + 1) * head, :]
    share_columns(crow, cr_ss, cr_rs)
    grad_t = crow[...].reshape(part, width).astype(F32).T.astype(BF16)
    for h in range(HEADS):
        low, high = (h % 2) * head, (h % 2 + 1) * head
        ctm[h, low:high, :] = grad_t[h * head:(h + 1) * head, :]
    for load in loads[5:]:
        load.wait()

    def terms(h, kp, vp, m):
        t = jnp.tanh(dot(kp, qtm[h]) * scale)
        e = m * jnp.exp(SCORE_BOUND * t)
        slope = e * ((1.0 - t * t) * inverse_root)
        return e, slope * dot(vp, ctm[h]), slope

    def weights_only(h, kp, m):
        return m * jnp.exp(SCORE_BOUND * jnp.tanh(dot(kp, qtm[h]) * scale))

    def forward(step, carry):
        k = flip(me_k, step, chunks)
        first = pl.multiple_of(k * block, block)

        @pl.when(step + 1 < chunks)
        def _():
            nxt = flip(me_k, step + 1, chunks)
            slot = nxt * per + side
            arrived(fcol, col_rs, col_rs, "rows", slot)
            remote(fcol.at[slot], fcol.at[slot], col_fs.at[nxt], col_rs.at[slot], "rows", twin_r).start()

        arrived(fcol, col_rs, col_rs, "rows", k * per + (1 - side))
        rows = fcol[pl.ds(k * per, per)].reshape(block, width)
        keyed = dot(rows, wk[...])
        k_s[pl.ds(first, block), :] = keyed.astype(BF16)
        kt_s[k] = keyed.T.astype(BF16)
        valued = dot(rows, wv[...])
        v_s[pl.ds(first, block), :] = valued.astype(BF16)
        vt_s[k] = valued.T.astype(BF16)

        def pair(p, inner):
            lanes = pl.ds(pl.multiple_of(p * LANES, LANES), LANES)
            kp = k_s[pl.ds(first, block), lanes]
            m = mask_t[pl.ds(first, block), :]
            for a in range(2):
                h = 2 * p + a
                if keep:
                    e, raised, slope = terms(h, kp, v_s[pl.ds(first, block), lanes], m)
                    e_s[h, pl.ds(first, block), :] = e
                    a_s[h, pl.ds(first, block), :] = raised
                    b_s[h, pl.ds(first, block), :] = slope
                else:
                    e = weights_only(h, kp, m)
                vt = vt_s[k, pl.ds(pl.multiple_of(h * head, head), head), :]
                num_t[h] += dot(vt, e.astype(BF16))
                den_s[h] += jnp.sum(e.reshape(block // 8, 8, part), axis=0)
            return inner

        lax.fori_loop(0, HEADS // 2, pair, 0)
        return carry

    lax.fori_loop(0, chunks, forward, 0)

    for h in range(HEADS):
        low, high = (h % 2) * head, (h % 2 + 1) * head
        stat_send[0, h:h + 1] = jnp.sum(den_s[h], axis=0, keepdims=True)
        stat_send[1, h:h + 1] = jnp.sum(num_t[h] * ctm[h, low:high, :].astype(F32), axis=0, keepdims=True)
    for peer in col_peers:
        send(stat_send, stat_recv.at[me_c], st_ss.at[peer], st_rs.at[me_c], "cols", peer)
    stat_recv[me_c] = stat_send[...]
    for peer in col_peers:
        arrived(stat_recv, st_ss, st_rs, "cols", peer)
    total = jnp.sum(stat_recv[...], axis=0)
    inverse = 1.0 / total[0]
    inv_s[...] = inverse
    dl_s[...] = total[1] * inverse

    out_part = (num_t[...] * inverse[:, None, :]).reshape(width, part).T
    num_send[...] = out_part.astype(BF16).reshape(col_total, owned, width)
    for peer in col_peers:
        send(num_send.at[peer], num_recv.at[me_c], nu_ss.at[peer], nu_rs.at[me_c], "cols", peer)
    num_recv[me_c] = num_send[me_c]

    lane = lax.broadcasted_iota(jnp.int32, (part, LANES), 1)

    def pass_on(k):
        arrived(tw_recv, tw_rs, tw_rs, "rows", k)
        rg_send[k] = (rg_own[k] + tw_recv[k].astype(F32)).astype(BF16)
        remote(
            rg_send.at[k], rg_recv.at[me_k], rg_ss.at[k], rg_rs.at[me_k], "rows", k * per + side
        ).start()

    def backward(step, carry):
        k = flip(me_k, chunks - 1 - step, chunks)
        first = pl.multiple_of(k * block, block)

        def pair(p, inner):
            lanes = pl.ds(pl.multiple_of(p * LANES, LANES), LANES)
            qp = q_s[:, lanes]
            cp = crow[:, :, lanes].reshape(part, LANES)
            kg = jnp.zeros((block, LANES), F32)
            vg = jnp.zeros((block, LANES), F32)
            for a in range(2):
                h = 2 * p + a
                here = pl.ds(first, block)
                if keep:
                    e, raised, slope = e_s[h, here, :], a_s[h, here, :], b_s[h, here, :]
                else:
                    e, raised, slope = terms(h, k_s[here, lanes], v_s[here, lanes], mask_t[here, :])
                inv = inv_s[pl.ds(h, 1), :]
                gb = ((raised - slope * dl_s[pl.ds(h, 1), :]) * inv).astype(BF16)
                sb = (e * inv).astype(BF16)
                mine = (lane >= a * head) & (lane < (a + 1) * head)
                kt = kt_s[k, pl.ds(pl.multiple_of(h * head, head), head), :]
                qg_t[h] += dot(kt, gb)
                kg += dot(gb, jnp.where(mine, qp, jnp.zeros_like(qp)))
                vg += dot(sb, jnp.where(mine, cp, jnp.zeros_like(cp)))
            kg_s[:, lanes] = kg.astype(BF16)
            vg_s[:, lanes] = vg.astype(BF16)
            return inner

        lax.fori_loop(0, HEADS // 2, pair, 0)
        theirs, mine = pl.ds((1 - side) * owned, owned), pl.ds(side * owned, owned)
        sums = dot_t(kg_s[theirs, :], wk[...]) + dot_t(vg_s[theirs, :], wv[...])
        tw_send[k] = sums.astype(BF16)
        remote(tw_send.at[k], tw_recv.at[k], tw_ss.at[k], tw_rs.at[k], "rows", twin_r).start()
        rg_own[k] = dot_t(kg_s[mine, :], wk[...]) + dot_t(vg_s[mine, :], wv[...])

        @pl.when(step > 0)
        def _():
            pass_on(flip(me_k, chunks - step, chunks))

        return carry

    lax.fori_loop(0, chunks, backward, 0)

    query_grad = qg_t[...].reshape(width, part).T.astype(BF16)
    qg_send[...] = dot_t(query_grad, wq[...]).astype(BF16).reshape(col_total, owned, width)
    for peer in col_peers:
        send(qg_send.at[peer], qg_recv.at[me_c], qg_ss.at[peer], qg_rs.at[me_c], "cols", peer)
    qg_recv[me_c] = qg_send[me_c]

    for peer in col_peers:
        arrived(num_recv, nu_ss, nu_rs, "cols", peer)
    att_out[...] = jnp.sum(num_recv[...].astype(F32), axis=0).astype(BF16)
    arrived(tw_recv, tw_rs, tw_rs, "rows", me_k)
    grad = rg_own[me_k] + tw_recv[me_k].astype(F32)
    for x in line:
        arrived(rg_recv, rg_ss, rg_rs, "rows", x)
        grad += rg_recv[x].astype(F32)
    for peer in col_peers:
        arrived(qg_recv, qg_ss, qg_rs, "cols", peer)
    grad_out[...] = grad + jnp.sum(qg_recv[...].astype(F32), axis=0)

    for copy in sends:
        copy.wait_send()
    remote(tw_send.at[me_k], tw_recv.at[me_k], tw_ss.at[me_k], tw_rs.at[me_k], "rows", twin_r).wait_send()
    for x in line:
        slot = x * per + side
        remote(fcol.at[slot], fcol.at[slot], col_fs.at[x], col_rs.at[slot], "rows", twin_r).wait_send()
        remote(tw_send.at[x], tw_recv.at[x], tw_ss.at[x], tw_rs.at[x], "rows", twin_r).wait_send()
        remote(rg_send.at[x], rg_recv.at[me_k], rg_ss.at[x], rg_rs.at[me_k], "rows", slot).wait_send()


def local(row_total, col_total, features, w_query, w_key, w_value, cotangent, block_pairs, pair_count, edge_mask):
    owned, width = features.shape
    slots, block = edge_mask.shape[2], edge_mask.shape[3]
    part = owned * col_total
    span = owned * row_total
    chunks = span // block
    head = width // HEADS
    keep = span <= 512
    kept = (HEADS, span, part) if keep else (1, 8, LANES)
    vmem = pl.BlockSpec(memory_space=pltpu.VMEM)
    hbm = pl.BlockSpec(memory_space=pl.ANY)
    smem = pl.BlockSpec(memory_space=pltpu.SMEM)

    def buf(*shape, dtype=BF16):
        return pltpu.VMEM(shape, dtype)

    by_col = buf(col_total, owned, width)
    by_line = buf(chunks, owned, width)
    by_head = buf(HEADS, head, part, dtype=F32)
    kept_buf = buf(*kept, dtype=F32)
    square = buf(width, width)
    col_sem = pltpu.SemaphoreType.DMA((col_total,))
    row_sem = pltpu.SemaphoreType.DMA((row_total,))
    line_sem = pltpu.SemaphoreType.DMA((chunks,))
    scratch = [
        square, square, square, buf(slots, block, block, dtype=jnp.int32),
        buf(row_total, owned, width), by_col, by_col,
        buf(span, width), buf(span, width),
        buf(chunks, width, block), buf(chunks, width, block),
        buf(part, width), buf(HEADS, LANES, part), buf(HEADS, LANES, part),
        buf(span, part, dtype=F32), kept_buf, kept_buf, kept_buf,
        by_head, buf(HEADS, 8, part, dtype=F32),
        buf(HEADS, part, dtype=F32), buf(HEADS, part, dtype=F32),
        by_head, buf(block, width), buf(block, width),
        buf(2, HEADS, part, dtype=F32), buf(col_total, 2, HEADS, part, dtype=F32),
        by_col, by_col, by_col, by_col,
        by_line, by_line, buf(chunks, owned, width, dtype=F32), by_line, by_line,
        pltpu.SemaphoreType.DMA((7,)),
        line_sem, line_sem, row_sem,
        col_sem, col_sem, col_sem, col_sem, col_sem, col_sem, col_sem, col_sem,
        col_sem, col_sem, line_sem, line_sem, line_sem, line_sem,
    ]
    return pl.pallas_call(
        functools.partial(kernel, row_total, col_total, keep),
        out_shape=(
            jax.ShapeDtypeStruct((owned, width), BF16),
            jax.ShapeDtypeStruct((owned, width), F32),
        ),
        in_specs=[hbm, hbm, hbm, hbm, hbm, smem, smem, hbm],
        out_specs=(vmem, vmem),
        scratch_shapes=scratch,
        compiler_params=pltpu.CompilerParams(
            collective_id=0, has_side_effects=True, vmem_limit_bytes=56 * 1024 * 1024
        ),
    )(
        features, w_query, w_key, w_value, cotangent,
        block_pairs.reshape(slots, 2), pair_count, edge_mask.reshape(slots, block, block),
    )


def solution(mesh):
    in_specs = (
        P(("rows", "cols"), None),
        P(),
        P(),
        P(),
        P(("rows", "cols"), None),
        P("rows", "cols", None, None),
        P("rows", "cols"),
        P("rows", "cols", None, None, None),
    )
    out_specs = (P(("rows", "cols"), None), P(("rows", "cols"), None))
    body = functools.partial(local, mesh.shape["rows"], mesh.shape["cols"])
    return jax.shard_map(body, mesh=mesh, in_specs=in_specs, out_specs=out_specs, check_vma=False)
```

time: 51.8 us -> 46.7 us (0.902)
  Pallas kernels: 46.8 us -> 41.7 us
    pallas_call x1, Pallas kernels: 46.8 us -> 41.7 us  [local(): pl.pallas_call(functools.partial(kernel, row_total, col_total, keep), out...]
    unnamed x7 -> x6, local copies, waits for them, and re-layouts: 2.93 us -> 2.84 us
where the time goes in v2:
time: 46.7 us; the launch traced here: 46.5 us
  Pallas kernels  41.7 us (89%)
  local copies, waits for them, and re-layouts  3.52 us (8%)
  between operations  1.3 us (3%)
    pallas_call x1, Pallas kernels, local(): pl.pallas_call(functools.partial(kernel, row_total, col_total, keep), out...  41.7 us
    unnamed x6, local copies, waits for them, and re-layouts  2.84 us

profile of v2, /device:TPU:0, one launch (start us, length us, event | category | flops | bytes accessed | tf_op | source)
XLA Modules:
  0.0 46.5 jit_solution(5503254923355376318)
XLA Ops:
  1.3 0.0 copy-start.1
  1.3 0.7 %copy-done.1 = s32[1,1,6,2]{2,3,1,0:T(2,128)S(1)} copy-done((s32[1,1,6,2]{2,3,1,0:T(2,128)S(1)}, s32[1,1,6,2]{2,3,1,0:T(2,128)}, u32[]{:S(2)}) %copy-start.1) | copy-done | bytes 72
  2.0 0.7 %copy.10.pairs = s32[6,2]{1,0:T(8,128)} copy(s32[6,2]{0,1:T(2,128)S(1)} %bitcast.3) | data formatting | bytes 96 | tf_op jit(solution)/shard_map/reshape | solution.py:377
  2.6 41.7 %shard_map.95 = (bf16[64,512]{1,0:T(8,128)(2,1)}, f32[64,512]{1,0:T(8,128)}) custom-call(bf16[64,512]{1,0:T(8,128)(2,1)} %feat.1, bf16[512,512]{1,0:T(8,128)(2,1)} %wq_in.1, bf16[512,512]{1,0:T(8,128)(2,1)} %wk_in.1, bf16[512,512]{1,0:T(8,128)(2,1)} %wv_in.1, bf16[64,512]{1,0:T(8,128)(2,1)} %cot.1, s32[6,2]{1,0:T(8,128)} %copy.10.pairs, ...), custom_call_target="tpu_custom_call" | custom-call | tf_op jit(solution)/shard_map/pallas_call | solution.py:363
  44.3 0.0 copy-start
  44.3 1.5 %copy.14 = bf16[64,512]{1,0:T(8,128)(2,1)} copy(bf16[64,512]{1,0:T(8,128)(2,1)} %get-tuple-element.4) | data formatting | bytes 131072
  45.8 0.0 copy-done
  45.8 0.7 %copy.15 = f32[64,512]{1,0:T(8,128)} copy(f32[64,512]{1,0:T(8,128)S(1)} %copy-done) | data formatting | bytes 262144
Async XLA Ops:
  1.3 0.7 %copy-start.1 = (s32[1,1,6,2]{2,3,1,0:T(2,128)S(1)}, s32[1,1,6,2]{2,3,1,0:T(2,128)}, u32[]{:S(2)}) copy-start(s32[1,1,6,2]{2,3,1,0:T(2,128)} %param.13) | copy-start | bytes 148
  44.3 1.5 %copy-start = (f32[64,512]{1,0:T(8,128)S(1)}, f32[64,512]{1,0:T(8,128)}, u32[]{:S(2)}) copy-start(f32[64,512]{1,0:T(8,128)} %get-tuple-element.5) | copy-start | bytes 393220

commit v3 on v2

--- a/solution.py
+++ b/solution.py
@@ -20,16 +20,12 @@
     return jnp.dot(a, b, preferred_element_type=F32)
 
 
-def dot_t(a, b):
-    return lax.dot_general(a, b, (((1,), (1,)), ((), ())), preferred_element_type=F32)
-
-
 def kernel(
     row_total, col_total, keep,
-    feat, wq_in, wk_in, wv_in, cot, pairs, count, mask_in,
+    feat, wq_in, wk_in, wv_in, cot, pairs_in, count_in, mask_in,
     att_out, grad_out,
-    wq, wk, wv, mask, fcol, frow, crow, k_s, v_s, kt_s, vt_s, q_s, qtm, ctm, mask_t, e_s, a_s, b_s,
-    num_t, den_s, inv_s, dl_s, qg_t, kg_s, vg_s,
+    pairs, count, wq, wk, wv, wqt, wkt, wvt, mask, fcol, frow, crow, k_s, v_s, kt_s, vt_s, q_s, qtm, ctm, mask_t, e_s, a_s, b_s,
+    num_t, den_s, inv_s, dl_s, qg_t, kg_s, vg_s, g_s, s_s, sums_s, turn_s,
     stat_send, stat_recv, num_send, num_recv, qg_send, qg_recv,
     tw_send, tw_recv, rg_own, rg_send, rg_recv,
     load_s, col_ss, col_fs, col_rs, fr_ss, fr_rs, cr_ss, cr_rs, st_ss, st_rs, nu_ss, nu_rs,
@@ -41,6 +37,7 @@
     part = owned * col_total
     row_blocks = part // block
     chunks = owned * row_total // block
+    wide = math.gcd(chunks, 2)
     per = block // owned
     me_r = lax.axis_index("rows")
     me_c = lax.axis_index("cols")
@@ -79,7 +76,7 @@
         pltpu.make_async_copy(src, dst, load_s.at[n])
         for n, (src, dst) in enumerate(
             [
-                (mask_in, mask), (feat, frow.at[me_c]), (feat, fcol.at[me_r]), (cot, crow.at[me_c]),
+                (mask_in, mask), (pairs_in, pairs), (count_in, count), (feat, frow.at[me_c]), (feat, fcol.at[me_r]), (cot, crow.at[me_c]),
                 (wq_in, wq), (wk_in, wk), (wv_in, wv),
             ]
         )
@@ -92,25 +89,6 @@
         pl.semaphore_signal(barrier, inc=1, device_id={"cols": peer}, device_id_type=MESH)
     for load in loads:
         load.start()
-    pl.semaphore_wait(barrier, chunks + col_total - 1)
-
-    sends = []
-
-    def send(*args):
-        copy = remote(*args)
-        copy.start()
-        sends.append(copy)
-
-    for peer in col_line:
-        send(feat, frow.at[me_c], fr_ss.at[peer], fr_rs.at[me_c], "cols", peer)
-    send(feat, fcol.at[me_r], col_fs.at[me_k], col_rs.at[me_r], "rows", twin_r)
-    for x in line:
-        send(feat, fcol.at[me_r], col_ss.at[x], col_rs.at[me_r], "rows", x * per + side)
-    send(feat, frow.at[me_c], fr_ss.at[me_c], fr_rs.at[me_c], "cols", twin_c)
-    for peer in col_line:
-        send(cot, crow.at[me_c], cr_ss.at[peer], cr_rs.at[me_c], "cols", peer)
-    send(cot, crow.at[me_c], cr_ss.at[me_c], cr_rs.at[me_c], "cols", twin_c)
-
     num_t[...] = jnp.zeros_like(num_t)
     den_s[...] = jnp.zeros_like(den_s)
     qg_t[...] = jnp.zeros_like(qg_t)
@@ -119,13 +97,14 @@
         qtm[h, other:other + head, :] = jnp.zeros((head, part), BF16)
         ctm[h, other:other + head, :] = jnp.zeros((head, part), BF16)
 
+    for load in loads[:3]:
+        load.wait()
     live_total = count[0, 0]
-    loads[0].wait()
 
     def mask_chunk(k, carry):
         for b in range(row_blocks):
             def find(s, found):
-                hit = (pairs[s, 0] == b) & (pairs[s, 1] == k) & (s < live_total)
+                hit = (pairs[0, 0, s, 0] == b) & (pairs[0, 0, s, 1] == k) & (s < live_total)
                 return jnp.where(hit, s, found)
 
             found = lax.fori_loop(0, slots, find, jnp.int32(-1), unroll=slots <= 8)
@@ -141,6 +120,25 @@
 
     lax.fori_loop(0, chunks, mask_chunk, 0)
 
+    pl.semaphore_wait(barrier, chunks + col_total - 1)
+
+    sends = []
+
+    def send(*args):
+        copy = remote(*args)
+        copy.start()
+        sends.append(copy)
+
+    for peer in col_line:
+        send(feat, frow.at[me_c], fr_ss.at[peer], fr_rs.at[me_c], "cols", peer)
+    send(feat, fcol.at[me_r], col_fs.at[me_k], col_rs.at[me_r], "rows", twin_r)
+    for x in line:
+        send(feat, fcol.at[me_r], col_ss.at[x], col_rs.at[me_r], "rows", x * per + side)
+    send(feat, frow.at[me_c], fr_ss.at[me_c], fr_rs.at[me_c], "cols", twin_c)
+    for peer in col_line:
+        send(cot, crow.at[me_c], cr_ss.at[peer], cr_rs.at[me_c], "cols", peer)
+    send(cot, crow.at[me_c], cr_ss.at[me_c], cr_rs.at[me_c], "cols", twin_c)
+
     def share_columns(buf, ss, rs):
         for peer in col_line:
             arrived(buf, ss, rs, "cols", peer)
@@ -148,9 +146,25 @@
         for peer in [twin_c] + col_cross:
             arrived(buf, ss, rs, "cols", peer)
 
-    for load in loads[1:5]:
+    for load in loads[3:]:
         load.wait()
+    for straight, turned in ((wq, wqt), (wk, wkt), (wv, wvt)):
+        turned[...] = straight[...].T
+    def collect(k):
+        arrived(fcol, col_rs, col_rs, "rows", k * per + (1 - side))
+
+    def relay(k):
+        slot = k * per + side
+        arrived(fcol, col_rs, col_rs, "rows", slot)
+        remote(fcol.at[slot], fcol.at[slot], col_fs.at[k], col_rs.at[slot], "rows", twin_r).start()
+
+    tile = wide * block
+    tiles = chunks // wide
+    me_t = lax.div(me_k, wide)
+
     share_columns(frow, fr_ss, fr_rs)
+    for w in range(1, wide):
+        relay(me_t * wide + lax.rem(me_k - me_t * wide + w, wide))
     query = dot(frow[...].reshape(part, width), wq[...])
     q_s[...] = query.astype(BF16)
     query_t = query.T.astype(BF16)
@@ -162,8 +176,6 @@
     for h in range(HEADS):
         low, high = (h % 2) * head, (h % 2 + 1) * head
         ctm[h, low:high, :] = grad_t[h * head:(h + 1) * head, :]
-    for load in loads[5:]:
-        load.wait()
 
     def terms(h, kp, vp, m):
         t = jnp.tanh(dot(kp, qtm[h]) * scale)
@@ -175,47 +187,50 @@
         return m * jnp.exp(SCORE_BOUND * jnp.tanh(dot(kp, qtm[h]) * scale))
 
     def forward(step, carry):
-        k = flip(me_k, step, chunks)
-        first = pl.multiple_of(k * block, block)
-
-        @pl.when(step + 1 < chunks)
+        g = flip(me_t, step, tiles)
+        first = pl.multiple_of(g * tile, tile)
+        here = pl.ds(first, tile)
+
+        @pl.when(step + 1 < tiles)
         def _():
-            nxt = flip(me_k, step + 1, chunks)
-            slot = nxt * per + side
-            arrived(fcol, col_rs, col_rs, "rows", slot)
-            remote(fcol.at[slot], fcol.at[slot], col_fs.at[nxt], col_rs.at[slot], "rows", twin_r).start()
-
-        arrived(fcol, col_rs, col_rs, "rows", k * per + (1 - side))
-        rows = fcol[pl.ds(k * per, per)].reshape(block, width)
+            nxt = flip(me_t, step + 1, tiles)
+            for w in range(wide):
+                relay(nxt * wide + w)
+
+        for w in range(wide):
+            collect(g * wide + w)
+        rows = fcol[pl.ds(g * wide * per, wide * per)].reshape(tile, width)
         keyed = dot(rows, wk[...])
-        k_s[pl.ds(first, block), :] = keyed.astype(BF16)
-        kt_s[k] = keyed.T.astype(BF16)
+        k_s[here, :] = keyed.astype(BF16)
+        keyed_t = keyed.T.astype(BF16)
+        for w in range(wide):
+            kt_s[g * wide + w] = keyed_t[:, w * block:(w + 1) * block]
         valued = dot(rows, wv[...])
-        v_s[pl.ds(first, block), :] = valued.astype(BF16)
-        vt_s[k] = valued.T.astype(BF16)
+        v_s[here, :] = valued.astype(BF16)
+        vt_s[g] = valued.T.astype(BF16)
 
         def pair(p, inner):
             lanes = pl.ds(pl.multiple_of(p * LANES, LANES), LANES)
-            kp = k_s[pl.ds(first, block), lanes]
-            m = mask_t[pl.ds(first, block), :]
+            kp = k_s[here, lanes]
+            m = mask_t[here, :]
             for a in range(2):
                 h = 2 * p + a
                 if keep:
-                    e, raised, slope = terms(h, kp, v_s[pl.ds(first, block), lanes], m)
-                    e_s[h, pl.ds(first, block), :] = e
-                    a_s[h, pl.ds(first, block), :] = raised
-                    b_s[h, pl.ds(first, block), :] = slope
+                    e, raised, slope = terms(h, kp, v_s[here, lanes], m)
+                    e_s[h, here, :] = e
+                    a_s[h, here, :] = raised
+                    b_s[h, here, :] = slope
                 else:
                     e = weights_only(h, kp, m)
-                vt = vt_s[k, pl.ds(pl.multiple_of(h * head, head), head), :]
+                vt = vt_s[g, pl.ds(pl.multiple_of(h * head, head), head), :]
                 num_t[h] += dot(vt, e.astype(BF16))
-                den_s[h] += jnp.sum(e.reshape(block // 8, 8, part), axis=0)
+                den_s[h] += jnp.sum(e.reshape(tile // 8, 8, part), axis=0)
             return inner
 
         lax.fori_loop(0, HEADS // 2, pair, 0)
         return carry
 
-    lax.fori_loop(0, chunks, forward, 0)
+    lax.fori_loop(0, tiles, forward, 0)
 
     for h in range(HEADS):
         low, high = (h % 2) * head, (h % 2 + 1) * head
@@ -224,18 +239,17 @@
     for peer in col_peers:
         send(stat_send, stat_recv.at[me_c], st_ss.at[peer], st_rs.at[me_c], "cols", peer)
     stat_recv[me_c] = stat_send[...]
+    num_part = num_t[...].reshape(width, part).T
+    num_send[...] = num_part.astype(BF16).reshape(col_total, owned, width)
+    for peer in col_peers:
+        send(num_send.at[peer], num_recv.at[me_c], nu_ss.at[peer], nu_rs.at[me_c], "cols", peer)
+    num_recv[me_c] = num_send[me_c]
     for peer in col_peers:
         arrived(stat_recv, st_ss, st_rs, "cols", peer)
     total = jnp.sum(stat_recv[...], axis=0)
     inverse = 1.0 / total[0]
     inv_s[...] = inverse
     dl_s[...] = total[1] * inverse
-
-    out_part = (num_t[...] * inverse[:, None, :]).reshape(width, part).T
-    num_send[...] = out_part.astype(BF16).reshape(col_total, owned, width)
-    for peer in col_peers:
-        send(num_send.at[peer], num_recv.at[me_c], nu_ss.at[peer], nu_rs.at[me_c], "cols", peer)
-    num_recv[me_c] = num_send[me_c]
 
     lane = lax.broadcasted_iota(jnp.int32, (part, LANES), 1)
 
@@ -246,10 +260,28 @@
             rg_send.at[k], rg_recv.at[me_k], rg_ss.at[k], rg_rs.at[me_k], "rows", k * per + side
         ).start()
 
-    def backward(step, carry):
-        k = flip(me_k, chunks - 1 - step, chunks)
-        first = pl.multiple_of(k * block, block)
-
+    def scores(k):
+        here = pl.ds(pl.multiple_of(k * block, block), block)
+
+        def pair(p, inner):
+            lanes = pl.ds(pl.multiple_of(p * LANES, LANES), LANES)
+            for a in range(2):
+                h = 2 * p + a
+                if keep:
+                    e, raised, slope = e_s[h, here, :], a_s[h, here, :], b_s[h, here, :]
+                else:
+                    e, raised, slope = terms(h, k_s[here, lanes], v_s[here, lanes], mask_t[here, :])
+                inv = inv_s[pl.ds(h, 1), :]
+                gb = ((raised - slope * dl_s[pl.ds(h, 1), :]) * inv).astype(BF16)
+                g_s[h] = gb
+                s_s[h] = (e * inv).astype(BF16)
+                kt = kt_s[k, pl.ds(pl.multiple_of(h * head, head), head), :]
+                qg_t[h] += dot(kt, gb)
+            return inner
+
+        lax.fori_loop(0, HEADS // 2, pair, 0)
+
+    def range_grads(k):
         def pair(p, inner):
             lanes = pl.ds(pl.multiple_of(p * LANES, LANES), LANES)
             qp = q_s[:, lanes]
@@ -258,29 +290,23 @@
             vg = jnp.zeros((block, LANES), F32)
             for a in range(2):
                 h = 2 * p + a
-                here = pl.ds(first, block)
-                if keep:
-                    e, raised, slope = e_s[h, here, :], a_s[h, here, :], b_s[h, here, :]
-                else:
-                    e, raised, slope = terms(h, k_s[here, lanes], v_s[here, lanes], mask_t[here, :])
-                inv = inv_s[pl.ds(h, 1), :]
-                gb = ((raised - slope * dl_s[pl.ds(h, 1), :]) * inv).astype(BF16)
-                sb = (e * inv).astype(BF16)
                 mine = (lane >= a * head) & (lane < (a + 1) * head)
-                kt = kt_s[k, pl.ds(pl.multiple_of(h * head, head), head), :]
-                qg_t[h] += dot(kt, gb)
-                kg += dot(gb, jnp.where(mine, qp, jnp.zeros_like(qp)))
-                vg += dot(sb, jnp.where(mine, cp, jnp.zeros_like(cp)))
+                kg += dot(g_s[h], jnp.where(mine, qp, jnp.zeros_like(qp)))
+                vg += dot(s_s[h], jnp.where(mine, cp, jnp.zeros_like(cp)))
             kg_s[:, lanes] = kg.astype(BF16)
             vg_s[:, lanes] = vg.astype(BF16)
             return inner
 
         lax.fori_loop(0, HEADS // 2, pair, 0)
-        theirs, mine = pl.ds((1 - side) * owned, owned), pl.ds(side * owned, owned)
-        sums = dot_t(kg_s[theirs, :], wk[...]) + dot_t(vg_s[theirs, :], wv[...])
-        tw_send[k] = sums.astype(BF16)
+        sums_s[...] = dot(kg_s[...], wkt[...]) + dot(vg_s[...], wvt[...])
+        tw_send[k] = sums_s[pl.ds((1 - side) * owned, owned), :].astype(BF16)
         remote(tw_send.at[k], tw_recv.at[k], tw_ss.at[k], tw_rs.at[k], "rows", twin_r).start()
-        rg_own[k] = dot_t(kg_s[mine, :], wk[...]) + dot_t(vg_s[mine, :], wv[...])
+        rg_own[k] = sums_s[pl.ds(side * owned, owned), :]
+
+    def backward(step, carry):
+        k = flip(me_k, chunks - 1 - step, chunks)
+        scores(k)
+        range_grads(k)
 
         @pl.when(step > 0)
         def _():
@@ -288,17 +314,22 @@
 
         return carry
 
-    lax.fori_loop(0, chunks, backward, 0)
-
+    lax.fori_loop(0, chunks - 1, backward, 0)
+    scores(me_k)
     query_grad = qg_t[...].reshape(width, part).T.astype(BF16)
-    qg_send[...] = dot_t(query_grad, wq[...]).astype(BF16).reshape(col_total, owned, width)
+    qg_send[...] = dot(query_grad, wqt[...]).astype(BF16).reshape(col_total, owned, width)
     for peer in col_peers:
         send(qg_send.at[peer], qg_recv.at[me_c], qg_ss.at[peer], qg_rs.at[me_c], "cols", peer)
     qg_recv[me_c] = qg_send[me_c]
-
+    if chunks > 1:
+        pass_on(flip(me_k, 1, chunks))
+    range_grads(me_k)
+
+    turn_s[...] = jnp.broadcast_to(inv_s[...][:, None, :], (HEADS, head, part)).reshape(width, part).T
     for peer in col_peers:
         arrived(num_recv, nu_ss, nu_rs, "cols", peer)
-    att_out[...] = jnp.sum(num_recv[...].astype(F32), axis=0).astype(BF16)
+    mine_inv = turn_s[pl.ds(pl.multiple_of(me_c * owned, owned), owned), :]
+    att_out[...] = (jnp.sum(num_recv[...].astype(F32), axis=0) * mine_inv).astype(BF16)
     arrived(tw_recv, tw_rs, tw_rs, "rows", me_k)
     grad = rg_own[me_k] + tw_recv[me_k].astype(F32)
     for x in line:
@@ -325,11 +356,11 @@
     span = owned * row_total
     chunks = span // block
     head = width // HEADS
+    wide = math.gcd(chunks, 2)
     keep = span <= 512
     kept = (HEADS, span, part) if keep else (1, 8, LANES)
     vmem = pl.BlockSpec(memory_space=pltpu.VMEM)
     hbm = pl.BlockSpec(memory_space=pl.ANY)
-    smem = pl.BlockSpec(memory_space=pltpu.SMEM)
 
     def buf(*shape, dtype=BF16):
         return pltpu.VMEM(shape, dtype)
@@ -343,19 +374,22 @@
     row_sem = pltpu.SemaphoreType.DMA((row_total,))
     line_sem = pltpu.SemaphoreType.DMA((chunks,))
     scratch = [
-        square, square, square, buf(slots, block, block, dtype=jnp.int32),
+        pltpu.SMEM(block_pairs.shape, jnp.int32), pltpu.SMEM(pair_count.shape, jnp.int32),
+        square, square, square, square, square, square, buf(slots, block, block, dtype=jnp.int32),
         buf(row_total, owned, width), by_col, by_col,
         buf(span, width), buf(span, width),
-        buf(chunks, width, block), buf(chunks, width, block),
+        buf(chunks, width, block), buf(chunks // wide, width, wide * block),
         buf(part, width), buf(HEADS, LANES, part), buf(HEADS, LANES, part),
         buf(span, part, dtype=F32), kept_buf, kept_buf, kept_buf,
         by_head, buf(HEADS, 8, part, dtype=F32),
         buf(HEADS, part, dtype=F32), buf(HEADS, part, dtype=F32),
         by_head, buf(block, width), buf(block, width),
+        buf(HEADS, block, part), buf(HEADS, block, part),
+        buf(block, width, dtype=F32), buf(part, width, dtype=F32),
         buf(2, HEADS, part, dtype=F32), buf(col_total, 2, HEADS, part, dtype=F32),
         by_col, by_col, by_col, by_col,
         by_line, by_line, buf(chunks, owned, width, dtype=F32), by_line, by_line,
-        pltpu.SemaphoreType.DMA((7,)),
+        pltpu.SemaphoreType.DMA((9,)),
         line_sem, line_sem, row_sem,
         col_sem, col_sem, col_sem, col_sem, col_sem, col_sem, col_sem, col_sem,
         col_sem, col_sem, line_sem, line_sem, line_sem, line_sem,
@@ -366,7 +400,7 @@
             jax.ShapeDtypeStruct((owned, width), BF16),
             jax.ShapeDtypeStruct((owned, width), F32),
         ),
-        in_specs=[hbm, hbm, hbm, hbm, hbm, smem, smem, hbm],
+        in_specs=[hbm] * 8,
         out_specs=(vmem, vmem),
         scratch_shapes=scratch,
         compiler_params=pltpu.CompilerParams(
@@ -374,7 +408,7 @@
         ),
     )(
         features, w_query, w_key, w_value, cotangent,
-        block_pairs.reshape(slots, 2), pair_count, edge_mask.reshape(slots, block, block),
+        block_pairs, pair_count, edge_mask.reshape(slots, block, block),
     )
 
 

time: 46.7 us -> 43.4 us (0.929)
  Pallas kernels: 41.7 us -> 38.4 us
    pallas_call x1, Pallas kernels: 41.7 us -> 38.4 us  [local(): pl.pallas_call(functools.partial(kernel, row_total, col_total, keep), out...]
    unnamed x6 -> x7, local copies, waits for them, and re-layouts: 2.84 us -> 3.52 us
    reshape x1 -> x0, local copies, waits for them, and re-layouts: 0.68 us -> none  [local(): block_pairs.reshape(slots, 2)]
where the time goes in v3:
time: 43.4 us; the launch traced here: 43.2 us
  Pallas kernels  38.4 us (88%)
  local copies, waits for them, and re-layouts  3.52 us (8%)
  between operations  1.3 us (3%)
    pallas_call x1, Pallas kernels, local(): pl.pallas_call(functools.partial(kernel, row_total, col_total, keep), out...  38.4 us
    unnamed x7, local copies, waits for them, and re-layouts  3.52 us

profile of v3, /device:TPU:0, one launch (start us, length us, event | category | flops | bytes accessed | tf_op | source)
XLA Modules:
  0.0 43.2 jit_solution(10510509399714208892)
XLA Ops:
  1.3 0.0 copy-start.1
  1.3 0.7 %copy-done.1 = s32[1,1,6,2]{2,3,1,0:T(2,128)S(1)} copy-done((s32[1,1,6,2]{2,3,1,0:T(2,128)S(1)}, s32[1,1,6,2]{2,3,1,0:T(2,128)}, u32[]{:S(2)}) %copy-start.1) | copy-done | bytes 72
  2.0 0.7 %copy.10.pairs_in = s32[1,1,6,2]{3,2,1,0:T(8,128)} copy(s32[1,1,6,2]{2,3,1,0:T(2,128)S(1)} %copy-done.1) | data formatting | bytes 96 | tf_op args[5]
  2.6 38.4 %shard_map.95 = (bf16[64,512]{1,0:T(8,128)(2,1)}, f32[64,512]{1,0:T(8,128)}) custom-call(bf16[64,512]{1,0:T(8,128)(2,1)} %feat.1, bf16[512,512]{1,0:T(8,128)(2,1)} %wq_in.1, bf16[512,512]{1,0:T(8,128)(2,1)} %wk_in.1, bf16[512,512]{1,0:T(8,128)(2,1)} %wv_in.1, bf16[64,512]{1,0:T(8,128)(2,1)} %cot.1, s32[1,1,6,2]{3,2,1,0:T(8,128)} %copy.10.pairs_in, ...), custom_call_target="tpu_custom_call" | custom-call | tf_op jit(solution)/shard_map/pallas_call | solution.py:397
  41.0 0.0 copy-start
  41.0 1.5 %copy.14 = bf16[64,512]{1,0:T(8,128)(2,1)} copy(bf16[64,512]{1,0:T(8,128)(2,1)} %get-tuple-element.4) | data formatting | bytes 131072
  42.5 0.0 copy-done
  42.5 0.7 %copy.15 = f32[64,512]{1,0:T(8,128)} copy(f32[64,512]{1,0:T(8,128)S(1)} %copy-done) | data formatting | bytes 262144
Async XLA Ops:
  1.3 0.7 %copy-start.1 = (s32[1,1,6,2]{2,3,1,0:T(2,128)S(1)}, s32[1,1,6,2]{2,3,1,0:T(2,128)}, u32[]{:S(2)}) copy-start(s32[1,1,6,2]{2,3,1,0:T(2,128)} %param.13) | copy-start | bytes 148
  41.0 1.5 %copy-start = (f32[64,512]{1,0:T(8,128)S(1)}, f32[64,512]{1,0:T(8,128)}, u32[]{:S(2)}) copy-start(f32[64,512]{1,0:T(8,128)} %get-tuple-element.5) | copy-start | bytes 393220

commit v4 on v3

--- a/solution.py
+++ b/solution.py
@@ -129,20 +129,22 @@
         copy.start()
         sends.append(copy)
 
+    for x in line:
+        send(feat, fcol.at[me_r], col_ss.at[x], col_rs.at[me_r], "rows", x * per + side)
     for peer in col_line:
         send(feat, frow.at[me_c], fr_ss.at[peer], fr_rs.at[me_c], "cols", peer)
     send(feat, fcol.at[me_r], col_fs.at[me_k], col_rs.at[me_r], "rows", twin_r)
-    for x in line:
-        send(feat, fcol.at[me_r], col_ss.at[x], col_rs.at[me_r], "rows", x * per + side)
     send(feat, frow.at[me_c], fr_ss.at[me_c], fr_rs.at[me_c], "cols", twin_c)
     for peer in col_line:
         send(cot, crow.at[me_c], cr_ss.at[peer], cr_rs.at[me_c], "cols", peer)
     send(cot, crow.at[me_c], cr_ss.at[me_c], cr_rs.at[me_c], "cols", twin_c)
 
-    def share_columns(buf, ss, rs):
+    def pass_columns(buf, ss, rs):
         for peer in col_line:
             arrived(buf, ss, rs, "cols", peer)
             send(buf.at[peer], buf.at[peer], ss.at[peer + 1 - 2 * side_c], rs.at[peer], "cols", twin_c)
+
+    def take_columns(buf, ss, rs):
         for peer in [twin_c] + col_cross:
             arrived(buf, ss, rs, "cols", peer)
 
@@ -162,16 +164,21 @@
     tiles = chunks // wide
     me_t = lax.div(me_k, wide)
 
-    share_columns(frow, fr_ss, fr_rs)
+    pass_columns(frow, fr_ss, fr_rs)
+    pass_columns(crow, cr_ss, cr_rs)
+    take_columns(frow, fr_ss, fr_rs)
     for w in range(1, wide):
         relay(me_t * wide + lax.rem(me_k - me_t * wide + w, wide))
+    if tiles > 1:
+        for w in range(wide):
+            relay(flip(me_t, 1, tiles) * wide + w)
     query = dot(frow[...].reshape(part, width), wq[...])
     q_s[...] = query.astype(BF16)
     query_t = query.T.astype(BF16)
     for h in range(HEADS):
         low, high = (h % 2) * head, (h % 2 + 1) * head
         qtm[h, low:high, :] = query_t[h * head:(h + 1) * head, :]
-    share_columns(crow, cr_ss, cr_rs)
+    take_columns(crow, cr_ss, cr_rs)
     grad_t = crow[...].reshape(part, width).astype(F32).T.astype(BF16)
     for h in range(HEADS):
         low, high = (h % 2) * head, (h % 2 + 1) * head
@@ -191,9 +198,9 @@
         first = pl.multiple_of(g * tile, tile)
         here = pl.ds(first, tile)
 
-        @pl.when(step + 1 < tiles)
+        @pl.when(step + 2 < tiles)
         def _():
-            nxt = flip(me_t, step + 1, tiles)
+            nxt = flip(me_t, step + 2, tiles)
             for w in range(wide):
                 relay(nxt * wide + w)
 

time: 43.4 us -> 43.4 us (level)
  no operation moved by 1% of the time
where the time goes in v4:
time: 43.4 us; the launch traced here: 43.2 us
  Pallas kernels  38.4 us (88%)
  local copies, waits for them, and re-layouts  3.52 us (8%)
  between operations  1.3 us (3%)
    pallas_call x1, Pallas kernels, local(): pl.pallas_call(functools.partial(kernel, row_total, col_total, keep), out...  38.4 us
    unnamed x7, local copies, waits for them, and re-layouts  3.52 us

profile of v4, /device:TPU:0, one launch (start us, length us, event | category | flops | bytes accessed | tf_op | source)
XLA Modules:
  0.0 43.2 jit_solution(14885389062008545823)
XLA Ops:
  1.3 0.0 copy-start.1
  1.3 0.7 %copy-done.1 = s32[1,1,6,2]{2,3,1,0:T(2,128)S(1)} copy-done((s32[1,1,6,2]{2,3,1,0:T(2,128)S(1)}, s32[1,1,6,2]{2,3,1,0:T(2,128)}, u32[]{:S(2)}) %copy-start.1) | copy-done | bytes 72
  2.0 0.7 %copy.10.pairs_in = s32[1,1,6,2]{3,2,1,0:T(8,128)} copy(s32[1,1,6,2]{2,3,1,0:T(2,128)S(1)} %copy-done.1) | data formatting | bytes 96 | tf_op args[5]
  2.6 38.4 %shard_map.95 = (bf16[64,512]{1,0:T(8,128)(2,1)}, f32[64,512]{1,0:T(8,128)}) custom-call(bf16[64,512]{1,0:T(8,128)(2,1)} %feat.1, bf16[512,512]{1,0:T(8,128)(2,1)} %wq_in.1, bf16[512,512]{1,0:T(8,128)(2,1)} %wk_in.1, bf16[512,512]{1,0:T(8,128)(2,1)} %wv_in.1, bf16[64,512]{1,0:T(8,128)(2,1)} %cot.1, s32[1,1,6,2]{3,2,1,0:T(8,128)} %copy.10.pairs_in, ...), custom_call_target="tpu_custom_call" | custom-call | tf_op jit(solution)/shard_map/pallas_call | solution.py:404
  41.1 0.0 copy-start
  41.1 1.5 %copy.14 = bf16[64,512]{1,0:T(8,128)(2,1)} copy(bf16[64,512]{1,0:T(8,128)(2,1)} %get-tuple-element.4) | data formatting | bytes 131072
  42.6 0.0 copy-done
  42.6 0.7 %copy.15 = f32[64,512]{1,0:T(8,128)} copy(f32[64,512]{1,0:T(8,128)S(1)} %copy-done) | data formatting | bytes 262144
Async XLA Ops:
  1.3 0.7 %copy-start.1 = (s32[1,1,6,2]{2,3,1,0:T(2,128)S(1)}, s32[1,1,6,2]{2,3,1,0:T(2,128)}, u32[]{:S(2)}) copy-start(s32[1,1,6,2]{2,3,1,0:T(2,128)} %param.13) | copy-start | bytes 148
  41.1 1.5 %copy-start = (f32[64,512]{1,0:T(8,128)S(1)}, f32[64,512]{1,0:T(8,128)}, u32[]{:S(2)}) copy-start(f32[64,512]{1,0:T(8,128)} %get-tuple-element.5) | copy-start | bytes 393220
